TPU v7x, 128 devices: a whole 4x4x4 slice. The times are simulated.
128 devices in a mesh: cell: 16 (over y, x), gene: 8 (over z, core).
Axes of the slice: x: 4, y: 4, z: 4, core: 2. Of those that a mesh axis runs over, the one named last changes fastest.
Arguments:
- expression: float32 [24576, 32768], P('cell', 'gene'), may hold values from -16 to 18, as said below
- tile_mask: int32 [96, 128], P('cell', 'gene'), may hold values from 0 to 1, as said below
- start: float32 [32768, 32], P('gene'), may hold values from -6 to 6
Outputs:
- alphas: float32 [2, 32, 32], replicated
- betas: float32 [2, 32, 32], replicated
- next_block: float32 [32768, 32], P('gene')
Inputs may be any that keep to these rules, and one draw needn't show every extreme that they name: expression: positive mean per gene with gene and cell scales and independent noise. `tile_mask`: each row of tiles belongs to one of 8 cell types and each column of tiles to one of 8 gene modules; a tile is 1 where its type expresses its module.
All inputs are finite; a program needn't handle non-finite values.
Results may differ from a plain program's by a relative error of at most 0.0024.
Values sent between devices are 32-bit elements; how exact they have to be, the bound alone decides.
A program may use at most 128 MiB of HBM per device.

v0:
```python
import math
import jax
import jax.numpy as jnp
from jax import lax
from jax.sharding import PartitionSpec as P

TILE = 256
STEPS = 2
highest = lax.Precision.HIGHEST


def transposed_dot(left, right):
    return lax.dot_general(
        left, right, (((0,), (0,)), ((), ())), precision=highest, preferred_element_type=jnp.float32
    )


def product(left, right):
    return jnp.dot(left, right, precision=highest, preferred_element_type=jnp.float32)


def finish(resid, gram):
    lower = jnp.linalg.cholesky(gram)
    fresh = lax.linalg.triangular_solve(lower, resid, left_side=False, lower=True, transpose_a=True)
    return (fresh, jnp.transpose(lower))


def expand_mask(expression, tile_mask):
    rows, width = expression.shape
    tiles = expression.reshape(tile_mask.shape[0], TILE, tile_mask.shape[1], TILE)
    return (tiles * tile_mask.astype(jnp.float32)[:, None, :, None]).reshape(rows, width)


def orthogonalize(image, current, older):
    projections = [transposed_dot(current, image)]
    if older is not None:
        projections.append(transposed_dot(older, image))
    summed = lax.psum(jnp.stack(projections), "gene")
    resid = image - product(current, summed[0])
    if older is not None:
        resid = resid - product(older, summed[1])
    gram = lax.psum(transposed_dot(resid, resid), "gene")
    fresh, beta = finish(resid, gram)
    return (fresh, summed[0], beta)


def per_device(expression, tile_mask, start):
    cell_count = lax.axis_size("cell")
    gene_count = lax.axis_size("gene")
    rows, width = expression.shape
    cells = rows * cell_count
    masked = expand_mask(expression, tile_mask)
    means = lax.psum(jnp.sum(masked, axis=0), "cell") / cells
    current = start
    gram_start = lax.psum(transposed_dot(current, current), "gene")
    current = finish(current, gram_start)[0]
    older = None
    alpha_list = []
    beta_list = []
    for step in range(STEPS):
        partial_side = product(masked, current) - product(means[None, :], current)
        cell_side = lax.psum(partial_side, "gene")
        image = lax.psum(transposed_dot(masked, cell_side) / cells, "cell")
        fresh, alpha, beta = orthogonalize(image, current, older)
        alpha_list.append(alpha)
        beta_list.append(beta)
        older = current
        current = fresh
    next_block = current * math.sqrt(width * gene_count)
    return (jnp.stack(alpha_list), jnp.stack(beta_list), next_block)


def solution(mesh):
    in_specs = (P("cell", "gene"), P("cell", "gene"), P("gene", None))
    out_specs = (P(), P(), P("gene", None))
    return jax.shard_map(
        per_device, mesh=mesh, in_specs=in_specs, out_specs=out_specs, check_vma=False
    )
```

profile of v0, /device:TPU:0, one launch (start us, length us, event | category | flops | bytes accessed | tf_op | source)
XLA Modules:
  0.0 673.6 jit_solution(17267883612236582695)
XLA Ops:
  7.2 0.7 convert_element_type.3
  8.0 0.3 copy-done
  8.2 0.6 fusion.14
  8.8 27.0 %psum.70 = f32[32,32]{0,1:T(8,128)S(1)} all-reduce(f32[32,32]{0,1:T(8,128)S(1)} %fusion.14), channel_id=1, replica_groups=mesh['cell'=16,'gene'=8] {'gene'}, use_global_device_ids=true, to_apply=%region_0.0 | all-reduce | flops 1024 | bytes 8192 | tf_op jit(solution)/shard_map/psum | solution.py:55
  35.9 2.9 cholesky.59
  38.8 0.6 compare_reduce_fusion.2
  39.4 0.7 fusion.1
  40.1 2.4 custom-call.7
  42.5 0.6 convolution_bitcast_fusion.2
  43.2 11.6 %mul.17 = f32[6,256,16,256]{3,2,1,0:T(8,128)} broadcast(f32[6,16]{1,0:T(8,128)S(1)} %convert_element_type.3), dimensions={0,2} | broadcast | bytes 25166208 | tf_op jit(solution)/shard_map/mul | solution.py:31
  54.8 27.6 %copy.16 = f32[192,8,16,256]{3,1,2,0:T(8,128)S(1)} copy(f32[192,8,16,256]{3,2,1,0:T(8,128)} %bitcast.98) | data formatting | bytes 50331648
  82.4 18.8 %fusion.13 = (f32[4096]{0:T(1024)S(1)}, f32[1536,4096]{1,0:T(8,128)}) fusion(f32[1536,4096]{1,0:T(8,128)} %param.6, f32[1536,4096]{1,0:T(8,128)S(1)} %bitcast.97), kind=kLoop, calls=%fused_computation.49 | loop fusion | flops 12578816 | bytes 75513856 | tf_op jit(solution)/shard_map/reduce_sum | solution.py:53
  101.1 74.6 %psum.71 = f32[4096]{0:T(1024)S(1)} all-reduce(f32[4096]{0:T(1024)S(1)} %get-tuple-element.8), channel_id=1, replica_groups=mesh['cell'=16,'gene'=8] {'cell'}, use_global_device_ids=true, to_apply=%region_4.7 | all-reduce | flops 4096 | bytes 32768 | tf_op jit(solution)/shard_map/psum | solution.py:53
  175.7 0.5 convolution_bitcast_fusion.7
  176.3 23.5 %convolution_subtract_fusion.4 = f32[1536,32]{1,0:T(8,128)} fusion(f32[1536,4096]{1,0:T(8,128)} %get-tuple-element.9, f32[4096,32]{0,1:T(8,128)S(1)} %convolution_bitcast_fusion.2, f32[32]{0:T(128)S(1)} %convolution_bitcast_fusion.7), kind=kOutput, calls=%fused_computation.10 | convolution fusion | flops 2415968256 | bytes 25886848 | tf_op jit(solution)/shard_map/dot_general | solution.py:19
  199.9 55.4 %all-reduce.5.cloned.1.call-done = f32[1536,32]{1,0:T(8,128)} async-done(((f32[1536,32]{1,0:T(8,128)}), f32[1536,32]{1,0:T(8,128)}) %all-reduce.5.cloned.1.call-update) | async-done | bytes 196624 | tf_op jit(solution)/shard_map/psum | solution.py:62
  255.3 18.8 %convolution_multiply_fusion.1 = f32[4096,32]{0,1:T(8,128)} fusion(f32[1536,4096]{1,0:T(8,128)} %get-tuple-element.9, f32[1536,32]{1,0:T(8,128)} %all-reduce.5.cloned.1.call-done), kind=kOutput, calls=%fused_computation.8 | convolution fusion | flops 2416050176 | bytes 25886720 | tf_op jit(solution)/shard_map/dot_general | solution.py:13
  274.2 84.2 %all-reduce.7.cloned.1.call-done = f32[4096,32]{0,1:T(8,128)} async-done(((f32[4096,32]{0,1:T(8,128)}), f32[4096,32]{0,1:T(8,128)}) %all-reduce.7.cloned.1.call-update) | async-done | bytes 524304 | tf_op jit(solution)/shard_map/psum | solution.py:63
  358.4 1.6 convolution_bitcast_fusion.5
  360.0 24.4 %psum.74 = f32[1,32,32]{2,1,0:T(8,128)S(1)} all-reduce(f32[1,32,32]{2,1,0:T(8,128)S(1)} %convolution_bitcast_fusion.5), channel_id=1, replica_groups=mesh['cell'=16,'gene'=8] {'gene'}, use_global_device_ids=true, to_apply=%region_7.10 | all-reduce | flops 1024 | bytes 8192 | tf_op jit(solution)/shard_map/psum | solution.py:38
  384.4 1.7 convolution_subtract_fusion.2
  386.0 0.6 fusion.15
  386.6 23.8 %psum.75 = f32[32,32]{0,1:T(8,128)S(1)} all-reduce(f32[32,32]{0,1:T(8,128)S(1)} %fusion.15), channel_id=1, replica_groups=mesh['cell'=16,'gene'=8] {'gene'}, use_global_device_ids=true, to_apply=%region_8.11 | all-reduce | flops 1024 | bytes 8192 | tf_op jit(solution)/shard_map/psum | solution.py:42
  410.5 2.9 cholesky.70
  413.4 0.6 compare_reduce_fusion.1
  414.1 0.7 fusion.10
  414.7 2.4 custom-call.8
  417.2 0.6 convolution_bitcast_fusion.1
  417.8 0.5 convolution_bitcast_fusion.6
  418.3 23.6 %convolution_subtract_fusion.3 = f32[1536,32]{1,0:T(8,128)} fusion(f32[1536,4096]{1,0:T(8,128)} %get-tuple-element.9, f32[4096,32]{0,1:T(8,128)S(1)} %convolution_bitcast_fusion.1, f32[32]{0:T(128)S(1)} %convolution_bitcast_fusion.6), kind=kOutput, calls=%fused_computation.9 | convolution fusion | flops 2415968256 | bytes 25886848 | tf_op jit(solution)/shard_map/dot_general | solution.py:19
  442.0 58.3 %all-reduce.9.cloned.1.call-done = f32[1536,32]{1,0:T(8,128)} async-done(((f32[1536,32]{1,0:T(8,128)}), f32[1536,32]{1,0:T(8,128)}) %all-reduce.9.cloned.1.call-update) | async-done | bytes 196624 | tf_op jit(solution)/shard_map/psum | solution.py:62
  500.3 18.8 %convolution_multiply_fusion = f32[4096,32]{0,1:T(8,128)} fusion(f32[1536,4096]{1,0:T(8,128)} %get-tuple-element.9, f32[1536,32]{1,0:T(8,128)} %all-reduce.9.cloned.1.call-done), kind=kOutput, calls=%fused_computation.7 | convolution fusion | flops 2416050176 | bytes 25886720 | tf_op jit(solution)/shard_map/dot_general | solution.py:13
  519.1 84.3 %all-reduce.11.cloned.1.call-done = f32[4096,32]{0,1:T(8,128)} async-done(((f32[4096,32]{0,1:T(8,128)}), f32[4096,32]{0,1:T(8,128)}) %all-reduce.11.cloned.1.call-update) | async-done | bytes 524304 | tf_op jit(solution)/shard_map/psum | solution.py:63
  603.4 1.6 convolution_bitcast_fusion.3
  605.0 1.6 convolution_bitcast_fusion.4
  606.6 24.5 %psum.78 = f32[2,32,32]{2,1,0:T(8,128)S(1)} all-reduce(f32[2,32,32]{2,1,0:T(8,128)S(1)} %pad_maximum_fusion), channel_id=1, replica_groups=mesh['cell'=16,'gene'=8] {'gene'}, use_global_device_ids=true, to_apply=%region_11.14 | all-reduce | flops 2048 | bytes 16384 | tf_op jit(solution)/shard_map/psum | solution.py:38
  631.1 1.7 convolution_subtract_fusion.1
  632.7 0.6 convolution_subtract_fusion
  633.4 0.6 pad_maximum_fusion.1
  634.0 0.6 fusion.16
  634.5 23.6 %psum.79 = f32[32,32]{0,1:T(8,128)S(1)} all-reduce(f32[32,32]{0,1:T(8,128)S(1)} %fusion.16), channel_id=1, replica_groups=mesh['cell'=16,'gene'=8] {'gene'}, use_global_device_ids=true, to_apply=%region_12.15 | all-reduce | flops 1024 | bytes 8192 | tf_op jit(solution)/shard_map/psum | solution.py:42
  658.1 0.1 copy.11
  658.2 2.9 cholesky.81
  661.1 0.6 compare_reduce_fusion
  661.8 0.7 select_bitcast_fusion
  662.4 2.4 custom-call.9
  664.9 1.4 fusion
  666.3 0.7 copy.12
  (23 shorter events, 0.5 us)
Async XLA Ops:
  7.2 1.1 copy-start
  7.2 248.1 %all-reduce.5.cloned.1.call-start = ((), (), s32[]{:S(2)}) async-start(), calls=%async_computation | async-start | bytes 1572864 | tf_op jit(solution)/shard_map/psum | solution.py:62
  199.8 158.6 %all-reduce.7.cloned.1.call-start = ((), (), s32[]{:S(2)}) async-start(), calls=%async_computation.1 | async-start | bytes 1048576 | tf_op jit(solution)/shard_map/psum | solution.py:63
  274.1 226.2 %all-reduce.9.cloned.1.call-start = ((), (), s32[]{:S(2)}) async-start(), calls=%async_computation.2 | async-start | bytes 1572864 | tf_op jit(solution)/shard_map/psum | solution.py:62
  418.3 248.7 %copy-start.1 = (f32[4096,32]{0,1:T(8,128)S(1)}, f32[4096,32]{0,1:T(8,128)}, u32[]{:S(2)}) copy-start(f32[4096,32]{0,1:T(8,128)} %param.8) | copy-start | bytes 1572868
  442.0 161.4 %all-reduce.11.cloned.1.call-start = ((), (), s32[]{:S(2)}) async-start(), calls=%async_computation.3 | async-start | bytes 1048576 | tf_op jit(solution)/shard_map/psum | solution.py:63
Sparse Core Ops, SparseCore 0:
  199.9 55.2 all-reduce.4
  274.2 84.0 all-reduce.6
  442.1 58.1 all-reduce.8
  519.2 84.0 all-reduce.10
where the time goes:
time: 674 us
  waiting for transfers between devices  282 us (42%)
  blocking collectives  198 us (29%)
  matrix products  98.9 us (15%)
  local copies, waits for them, and re-layouts  40.4 us (6%)
  other arithmetic  40.2 us (6%)
  between operations  13.9 us (2%)
    psum x2, waiting for transfers between devices, per_device(): image = lax.psum(transposed_dot(masked, cell_side) / cells, 'cell')  168 us
    psum x2, waiting for transfers between devices, per_device(): cell_side = lax.psum(partial_side, 'gene')  114 us
    psum x1, blocking collectives, per_device(): means = lax.psum(jnp.sum(masked, axis=0), 'cell') / cells  74.6 us
    dot_general x7, matrix products, product(): jnp.dot(left, right, precision=highest, preferred_element_type=jnp.float32)  52.1 us
    psum x2, blocking collectives, orthogonalize(): summed = lax.psum(jnp.stack(projections), 'gene')  48.9 us
    psum x2, blocking collectives, orthogonalize(): gram = lax.psum(transposed_dot(resid, resid), 'gene')  47.3 us
    dot_general x8, matrix products, transposed_dot(): lax.dot_general(left, right, (((0,), (0,)), ((), ())), precision=highest,...  44.1 us
    unnamed x6, local copies, waits for them, and re-layouts  28.6 us
  transfers between devices with their start and end apart: 4, of which 4 were waited for; matrix products, arithmetic and copies ran while one was open for 0% of the time, Pallas kernels for 0%

commit v1 on v0

--- a/solution.py
+++ b/solution.py
@@ -1,3 +1,4 @@
+import functools
 import math
 import jax
 import jax.numpy as jnp
@@ -7,6 +8,21 @@
 TILE = 256
 STEPS = 2
 highest = lax.Precision.HIGHEST
+
+
+def pack_sector_by_axis(target, mesh_name):
+    z, ready = (target, 0)
+    axis_total = jax.lax.axis_size(mesh_name)
+    while 1 << ready < axis_total:
+        kept_arr = jax.lax.ppermute(
+            z, mesh_name, tuple(((dev, dev ^ 1 << ready) for dev in range(axis_total)))
+        )
+        z = z + kept_arr
+        ready = ready + 1
+    return z
+
+
+group_the_sources_all = functools.partial(pack_sector_by_axis, mesh_name="gene")
 
 
 def transposed_dot(left, right):
@@ -59,7 +75,7 @@
     beta_list = []
     for step in range(STEPS):
         partial_side = product(masked, current) - product(means[None, :], current)
-        cell_side = lax.psum(partial_side, "gene")
+        cell_side = group_the_sources_all(partial_side)
         image = lax.psum(transposed_dot(masked, cell_side) / cells, "cell")
         fresh, alpha, beta = orthogonalize(image, current, older)
         alpha_list.append(alpha)

time: 674 us -> 601 us (0.89); the launches traced: 674 us -> 593 us
  waiting for transfers between devices: 282 us -> 192 us
  matrix products: 98.9 us -> 107 us
    psum x2 -> x0, waiting for transfers between devices: 114 us -> none  [per_device(): cell_side = lax.psum(partial_side, 'gene')]
    ppermute x0 -> x6, waiting for transfers between devices: none -> 31.9 us  [pack_sector_by_axis(): jax.lax.ppermute(z, mesh_name, tuple(((dev, dev ^ 1 << ready) for dev in...]
    psum x2, waiting for transfers between devices: 168 us -> 160 us  [per_device(): image = lax.psum(transposed_dot(masked, cell_side) / cells, 'cell')]
  transfers between devices with their start and end apart: 4 -> 8, of which waited for: 4 -> 8; matrix products, arithmetic and copies ran while one was open for 0% -> 0% of each run, Pallas kernels for 0% -> 0%
where the time goes in v1:
time: 601 us; the launch traced here: 593 us
  blocking collectives  198 us (33%)
  waiting for transfers between devices  192 us (32%)
  matrix products  107 us (18%)
  local copies, waits for them, and re-layouts  40.4 us (7%)
  other arithmetic  40.3 us (7%)
  between operations  14.5 us (2%)
    psum x2, waiting for transfers between devices, per_device(): image = lax.psum(transposed_dot(masked, cell_side) / cells, 'cell')  160 us
    psum x1, blocking collectives, per_device(): means = lax.psum(jnp.sum(masked, axis=0), 'cell') / cells  75.1 us
    dot_general x7, matrix products, product(): jnp.dot(left, right, precision=highest, preferred_element_type=jnp.float32)  57.8 us
    psum x2, blocking collectives, orthogonalize(): summed = lax.psum(jnp.stack(projections), 'gene')  48.9 us
    psum x2, blocking collectives, orthogonalize(): gram = lax.psum(transposed_dot(resid, resid), 'gene')  47.1 us
    dot_general x8, matrix products, transposed_dot(): lax.dot_general(left, right, (((0,), (0,)), ((), ())), precision=highest,...  46.3 us
    ppermute x6, waiting for transfers between devices, pack_sector_by_axis(): jax.lax.ppermute(z, mesh_name, tuple(((dev, dev ^ 1 << ready) for dev in...  31.9 us
    unnamed x6, local copies, waits for them, and re-layouts  28.6 us
  transfers between devices with their start and end apart: 8, of which 8 were waited for; matrix products, arithmetic and copies ran while one was open for 0% of the time, Pallas kernels for 0%

profile of v1, /device:TPU:0, one launch (start us, length us, event | category | flops | bytes accessed | tf_op | source)
XLA Modules:
  0.0 593.4 jit_solution(15973040228173182259)
XLA Ops:
  7.2 0.7 convert_element_type.3
  8.2 0.6 fusion.16
  8.8 27.0 %psum.56 = f32[32,32]{0,1:T(8,128)S(1)} all-reduce(f32[32,32]{0,1:T(8,128)S(1)} %fusion.16), channel_id=1, replica_groups=mesh['cell'=16,'gene'=8] {'gene'}, use_global_device_ids=true, to_apply=%region_0.0 | all-reduce | flops 1024 | bytes 8192 | tf_op jit(solution)/shard_map/psum | solution.py:71
  35.9 2.9 cholesky.59
  38.8 0.6 compare_reduce_fusion.2
  39.5 0.7 fusion.3
  40.1 2.4 custom-call.7
  42.5 0.6 convolution_bitcast_fusion.2
  43.2 11.6 %mul.17 = f32[6,256,16,256]{3,2,1,0:T(8,128)} broadcast(f32[6,16]{1,0:T(8,128)S(1)} %convert_element_type.3), dimensions={0,2} | broadcast | bytes 25166208 | tf_op jit(solution)/shard_map/mul | solution.py:47
  54.8 27.6 %copy.16 = f32[192,8,16,256]{3,1,2,0:T(8,128)S(1)} copy(f32[192,8,16,256]{3,2,1,0:T(8,128)} %bitcast.96) | data formatting | bytes 50331648
  82.4 18.8 %fusion.15 = (f32[4096]{0:T(1024)S(1)}, f32[1536,4096]{1,0:T(8,128)}) fusion(f32[1536,4096]{1,0:T(8,128)} %param.6, f32[1536,4096]{1,0:T(8,128)S(1)} %bitcast.95), kind=kLoop, calls=%fused_computation.51 | loop fusion | flops 12578816 | bytes 75513856 | tf_op jit(solution)/shard_map/reduce_sum | solution.py:69
  101.1 75.1 %psum.57 = f32[4096]{0:T(1024)S(1)} all-reduce(f32[4096]{0:T(1024)S(1)} %get-tuple-element.8), channel_id=1, replica_groups=mesh['cell'=16,'gene'=8] {'cell'}, use_global_device_ids=true, to_apply=%region_4.7 | all-reduce | flops 4096 | bytes 32768 | tf_op jit(solution)/shard_map/psum | solution.py:69
  176.8 26.4 %convolution_subtract_fusion.4 = f32[1536,32]{0,1:T(8,128)S(1)} fusion(f32[1536,4096]{1,0:T(8,128)} %get-tuple-element.9, f32[4096,32]{0,1:T(8,128)S(1)} %convolution_bitcast_fusion.2, f32[32]{0:T(128)S(1)} %convolution_bitcast_fusion.7), kind=kOutput, calls=%fused_computation.10 | convolution fusion | flops 2415968256 | bytes 25886848 | tf_op jit(solution)/shard_map/dot_general | solution.py:35
  203.3 1.4 collective-permute-done
  204.8 6.9 %collective-permute-done.1 = f32[1536,32]{0,1:T(8,128)S(1)} collective-permute-done((f32[1536,32]{0,1:T(8,128)S(1)}, f32[1536,32]{0,1:T(8,128)S(1)}, u32[]{:S(2)}, u32[]{:S(2)}) %collective-permute-start.1) | collective-permute-done | bytes 196640 | tf_op jit(solution)/shard_map/ppermute | solution.py:17
  211.9 7.6 %collective-permute-done.2 = f32[1536,32]{0,1:T(8,128)S(1)} collective-permute-done((f32[1536,32]{0,1:T(8,128)S(1)}, f32[1536,32]{0,1:T(8,128)S(1)}, u32[]{:S(2)}, u32[]{:S(2)}) %collective-permute-start.2) | collective-permute-done | bytes 196640 | tf_op jit(solution)/shard_map/ppermute | solution.py:17
  219.5 19.9 %convolution_multiply_fusion.1 = f32[4096,32]{0,1:T(8,128)} fusion(f32[1536,4096]{1,0:T(8,128)} %get-tuple-element.9, f32[1536,32]{0,1:T(8,128)S(1)} %add.43, f32[1536,32]{0,1:T(8,128)S(1)} %collective-permute-done.2), kind=kOutput, calls=%fused_computation.8 | convolution fusion | flops 2416099328 | bytes 26083328 | tf_op jit(solution)/shard_map/dot_general | solution.py:29
  239.7 78.7 %all-reduce.3.cloned.1.call-done = f32[4096,32]{0,1:T(8,128)} async-done(((f32[4096,32]{0,1:T(8,128)}), f32[4096,32]{0,1:T(8,128)}) %all-reduce.3.cloned.1.call-update) | async-done | bytes 524304 | tf_op jit(solution)/shard_map/psum | solution.py:79
  318.4 1.6 convolution_bitcast_fusion.5
  320.0 24.4 %psum.59 = f32[1,32,32]{2,1,0:T(8,128)S(1)} all-reduce(f32[1,32,32]{2,1,0:T(8,128)S(1)} %convolution_bitcast_fusion.5), channel_id=1, replica_groups=mesh['cell'=16,'gene'=8] {'gene'}, use_global_device_ids=true, to_apply=%region_6.9 | all-reduce | flops 1024 | bytes 8192 | tf_op jit(solution)/shard_map/psum | solution.py:54
  344.5 1.7 convolution_subtract_fusion.2
  346.1 0.6 fusion.17
  346.7 23.6 %psum.60 = f32[32,32]{0,1:T(8,128)S(1)} all-reduce(f32[32,32]{0,1:T(8,128)S(1)} %fusion.17), channel_id=1, replica_groups=mesh['cell'=16,'gene'=8] {'gene'}, use_global_device_ids=true, to_apply=%region_7.10 | all-reduce | flops 1024 | bytes 8192 | tf_op jit(solution)/shard_map/psum | solution.py:58
  370.3 2.9 cholesky.70
  373.3 0.6 compare_reduce_fusion.1
  373.9 0.7 fusion.12
  374.6 2.4 custom-call.8
  377.0 0.7 convolution_bitcast_fusion.1
  378.2 26.4 %convolution_subtract_fusion.3 = f32[1536,32]{0,1:T(8,128)S(1)} fusion(f32[1536,4096]{1,0:T(8,128)} %get-tuple-element.9, f32[4096,32]{0,1:T(8,128)S(1)} %convolution_bitcast_fusion.1, f32[32]{0:T(128)S(1)} %convolution_bitcast_fusion.6), kind=kOutput, calls=%fused_computation.9 | convolution fusion | flops 2415968256 | bytes 25886848 | tf_op jit(solution)/shard_map/dot_general | solution.py:35
  404.7 1.4 collective-permute-done.3
  406.3 6.9 %collective-permute-done.4 = f32[1536,32]{0,1:T(8,128)S(1)} collective-permute-done((f32[1536,32]{0,1:T(8,128)S(1)}, f32[1536,32]{0,1:T(8,128)S(1)}, u32[]{:S(2)}, u32[]{:S(2)}) %collective-permute-start.4) | collective-permute-done | bytes 196640 | tf_op jit(solution)/shard_map/ppermute | solution.py:17
  413.6 7.6 %collective-permute-done.5 = f32[1536,32]{0,1:T(8,128)S(1)} collective-permute-done((f32[1536,32]{0,1:T(8,128)S(1)}, f32[1536,32]{0,1:T(8,128)S(1)}, u32[]{:S(2)}, u32[]{:S(2)}) %collective-permute-start.5) | collective-permute-done | bytes 196640 | tf_op jit(solution)/shard_map/ppermute | solution.py:17
  421.2 20.0 %convolution_multiply_fusion = f32[4096,32]{0,1:T(8,128)} fusion(f32[1536,4096]{1,0:T(8,128)} %get-tuple-element.9, f32[1536,32]{0,1:T(8,128)S(1)} %add.46, f32[1536,32]{0,1:T(8,128)S(1)} %collective-permute-done.5), kind=kOutput, calls=%fused_computation.7 | convolution fusion | flops 2416099328 | bytes 26083328 | tf_op jit(solution)/shard_map/dot_general | solution.py:29
  441.1 81.5 %all-reduce.5.cloned.1.call-done = f32[4096,32]{0,1:T(8,128)} async-done(((f32[4096,32]{0,1:T(8,128)}), f32[4096,32]{0,1:T(8,128)}) %all-reduce.5.cloned.1.call-update) | async-done | bytes 524304 | tf_op jit(solution)/shard_map/psum | solution.py:79
  522.7 1.6 convolution_bitcast_fusion.3
  524.3 1.6 convolution_bitcast_fusion.4
  525.9 24.4 %psum.62 = f32[2,32,32]{2,1,0:T(8,128)S(1)} all-reduce(f32[2,32,32]{2,1,0:T(8,128)S(1)} %pad_maximum_fusion), channel_id=1, replica_groups=mesh['cell'=16,'gene'=8] {'gene'}, use_global_device_ids=true, to_apply=%region_9.12 | all-reduce | flops 2048 | bytes 16384 | tf_op jit(solution)/shard_map/psum | solution.py:54
  550.3 1.7 convolution_subtract_fusion.1
  552.0 0.6 convolution_subtract_fusion
  552.6 0.6 pad_maximum_fusion.1
  553.2 0.6 fusion.18
  553.8 23.6 %psum.63 = f32[32,32]{0,1:T(8,128)S(1)} all-reduce(f32[32,32]{0,1:T(8,128)S(1)} %fusion.18), channel_id=1, replica_groups=mesh['cell'=16,'gene'=8] {'gene'}, use_global_device_ids=true, to_apply=%region_10.13 | all-reduce | flops 1024 | bytes 8192 | tf_op jit(solution)/shard_map/psum | solution.py:58
  577.4 2.9 cholesky.81
  580.4 0.6 compare_reduce_fusion
  581.0 0.7 select_bitcast_fusion
  581.7 2.4 custom-call.9
  584.1 1.4 fusion
  585.6 0.7 copy.12
  (33 shorter events, 2.8 us)
Async XLA Ops:
  7.2 1.1 copy-start
  7.2 311.3 %all-reduce.3.cloned.1.call-start = ((), (), s32[]{:S(2)}) async-start(), calls=%async_computation | async-start | bytes 1048576 | tf_op jit(solution)/shard_map/psum | solution.py:79
  203.2 1.5 collective-permute-start
  204.8 7.0 %collective-permute-start.1 = (f32[1536,32]{0,1:T(8,128)S(1)}, f32[1536,32]{0,1:T(8,128)S(1)}, u32[]{:S(2)}, u32[]{:S(2)}) collective-permute-start(f32[1536,32]{0,1:T(8,128)S(1)} %add.42), channel_id=1, source_target_pairs={{0,2},{1,3},{2,0},{3,1},{4,6},{5,7},{6,4},{7,5},{8,10},{9,11},{10,... | collective-permute-start | bytes 589832 | tf_op jit(solution)/shard_map/ppermute | solution.py:17
  211.8 7.7 %collective-permute-start.2 = (f32[1536,32]{0,1:T(8,128)S(1)}, f32[1536,32]{0,1:T(8,128)S(1)}, u32[]{:S(2)}, u32[]{:S(2)}) collective-permute-start(f32[1536,32]{0,1:T(8,128)S(1)} %add.43), channel_id=1, source_target_pairs={{0,4},{1,5},{2,6},{3,7},{4,0},{5,1},{6,2},{7,3},{8,12},{9,13},{10,... | collective-permute-start | bytes 589832 | tf_op jit(solution)/shard_map/ppermute | solution.py:17
  239.5 283.2 %all-reduce.5.cloned.1.call-start = ((), (), s32[]{:S(2)}) async-start(), calls=%async_computation.1 | async-start | bytes 1048576 | tf_op jit(solution)/shard_map/psum | solution.py:79
  378.2 208.1 %copy-start.1 = (f32[4096,32]{0,1:T(8,128)S(1)}, f32[4096,32]{0,1:T(8,128)}, u32[]{:S(2)}) copy-start(f32[4096,32]{0,1:T(8,128)} %param.8) | copy-start | bytes 1572868
  404.6 1.5 collective-permute-start.3
  406.2 7.0 %collective-permute-start.4 = (f32[1536,32]{0,1:T(8,128)S(1)}, f32[1536,32]{0,1:T(8,128)S(1)}, u32[]{:S(2)}, u32[]{:S(2)}) collective-permute-start(f32[1536,32]{0,1:T(8,128)S(1)} %add.45), channel_id=1, source_target_pairs={{0,2},{1,3},{2,0},{3,1},{4,6},{5,7},{6,4},{7,5},{8,10},{9,11},{10,... | collective-permute-start | bytes 589832 | tf_op jit(solution)/shard_map/ppermute | solution.py:17
  413.2 7.9 %collective-permute-start.5 = (f32[1536,32]{0,1:T(8,128)S(1)}, f32[1536,32]{0,1:T(8,128)S(1)}, u32[]{:S(2)}, u32[]{:S(2)}) collective-permute-start(f32[1536,32]{0,1:T(8,128)S(1)} %add.46), channel_id=1, source_target_pairs={{0,4},{1,5},{2,6},{3,7},{4,0},{5,1},{6,2},{7,3},{8,12},{9,13},{10,... | collective-permute-start | bytes 589832 | tf_op jit(solution)/shard_map/ppermute | solution.py:17
Sparse Core Ops, SparseCore 0:
  239.6 78.7 all-reduce.2
  441.3 81.3 all-reduce.4
